TPU v7x, 32 devices: a whole 2x2x4 slice. The times are simulated.
32 devices in a mesh: sec: 16 (over z, x, core), term: 2 (over y).
Axes of the slice: x: 2, y: 2, z: 4, core: 2. Of those that a mesh axis runs over, the one named last changes fastest.
Arguments:
- wavefunction: bfloat16 [64, 128, 2048], P('sec', None, 'term'), may hold values from -6 to 6
- sketch: float32 [64, 128, 32], P('sec'), may hold values from -6 to 6
- kept: int32 [64], P('sec'), may hold values from 8 to 32, as said below
- left_ids: int32 [2048], P(('sec', 'term')), may hold values from 0 to 63, as said below
- right_ids: int32 [2048], P(('sec', 'term')), may hold values from 0 to 63, as said below
- operators: bfloat16 [2048, 128, 128], P(('sec', 'term')), may hold values from -6 to 6
Outputs:
- rotation: bfloat16 [64, 128, 32], P('sec')
- renormalized: float32 [2048, 32, 32], P(('sec', 'term'))
Inputs may be any that keep to these rules, and one draw needn't show every extreme that they name: `kept`: at least 8; some sector keeps exactly 32. `left_ids`: block b's left sector is one of the 4 sectors held by sec index b // (64 * 2). `right_ids`: among the 64 blocks of one device (aligned blocks of 64 rows), at most 4 have their right sector among the 4 sectors of any one sec index, and some sec index gets exactly 4 of them.
All inputs are finite; a program needn't handle non-finite values.
Results may differ from a plain program's by a relative error of at most 0.0059.
Values may be sent and summed in bfloat16 or wider, within the bound.
A program may use at most 64 MiB of HBM per device.

v0:
```python
import jax
import jax.numpy as jnp
from jax import lax
from jax.sharding import PartitionSpec as P

HIGH = lax.Precision.HIGHEST


def orthonormal(range_block, lower_block):
    return lax.linalg.triangular_solve(
        lower_block, range_block, left_side=False, lower=True, transpose_a=True
    )


def finish(ranged, kept, column):
    gram = jnp.einsum("smk,sml->skl", ranged, ranged, precision=HIGH)
    lower = jnp.linalg.cholesky(gram)
    basis = jax.vmap(orthonormal)(ranged, lower)
    basis = jnp.where(column[None, None, :] < kept[:, None, None], basis, 0.0)
    return basis.astype(jnp.bfloat16)


def shards(wavefunction, sketch, kept, left_ids, right_ids, operators):
    sec_count = wavefunction.shape[0]
    width = sketch.shape[2]
    column = jnp.arange(width, dtype=jnp.int32)
    partial_density = jnp.einsum(
        "smr,snr->smn", wavefunction, wavefunction, preferred_element_type=jnp.float32
    )
    density = lax.psum(partial_density, "term")
    ranged = jnp.einsum("smn,snk->smk", density, sketch, precision=HIGH)
    rotation = finish(ranged, kept, column)
    local_left = left_ids - lax.axis_index("sec") * sec_count
    left_rot = rotation[local_left]
    every_rot = lax.all_gather(rotation, "sec", axis=0, tiled=True)
    right_rot = every_rot[right_ids]
    half = jnp.einsum(
        "bmk,bmn->bkn", left_rot, operators, preferred_element_type=jnp.float32
    ).astype(jnp.bfloat16)
    result = jnp.einsum("bkn,bnl->bkl", half, right_rot, preferred_element_type=jnp.float32)
    return (rotation, result)


def solution(mesh):
    in_specs = (
        P("sec", None, "term"),
        P("sec", None, None),
        P("sec"),
        P(("sec", "term")),
        P(("sec", "term")),
        P(("sec", "term"), None, None),
    )
    out_specs = (P("sec", None, None), P(("sec", "term"), None, None))
    return jax.shard_map(shards, mesh=mesh, in_specs=in_specs, out_specs=out_specs, check_vma=False)
```

profile of v0, /device:TPU:1, one launch (start us, length us, event | category | flops | bytes accessed | tf_op | source)
XLA Modules:
  0.0 98.1 jit_solution(17886027295928150168)
XLA Ops:
  7.2 0.0 copy-start
  7.2 0.0 copy-start.3
  7.2 0.0 copy-start.4
  7.2 0.0 copy-start.5
  7.2 0.0 copy-start.2
  7.2 0.0 all-reduce.2.cloned.1.call-start
  7.3 2.8 %fusion.4 = f32[4,128,128]{2,1,0:T(8,128)} fusion(bf16[4,128,1024]{2,1,0:T(8,128)(2,1)} %param.6), kind=kOutput, calls=%fused_computation.19 | convolution fusion | flops 134217728 | bytes 1310720 | tf_op jit(solution)/shard_map/smr,snr->smn/dot_general | solution.py:27
  10.1 0.0 all-reduce.2.cloned.1.call-update
  10.2 0.1 iota_compare_fusion.2
  10.3 25.5 %all-reduce.2.cloned.1.call-done = f32[4,128,128]{2,1,0:T(8,128)} async-done(((f32[4,128,128]{2,1,0:T(8,128)}), f32[4,128,128]{2,1,0:T(8,128)}) %all-reduce.2.cloned.1.call-update) | async-done | bytes 262160 | tf_op jit(solution)/shard_map/psum | solution.py:30
  35.8 1.5 %fusion.5 = f32[4,128,32]{1,2,0:T(8,128)S(1)} fusion(f32[4,128,128]{2,1,0:T(8,128)} %all-reduce.2.cloned.1.call-done, f32[4,128,32]{1,2,0:T(8,128)S(1)} %copy-done.2), kind=kOutput, calls=%fused_computation.20 | convolution fusion | flops 25165824 | bytes 393216 | tf_op jit(solution)/shard_map/smn,snk->smk/dot_general | solution.py:31
  37.2 0.2 fusion.6
  37.5 0.1 copy.14
  37.6 11.7 %custom-call.7 = f32[4,32,32]{2,1,0:T(8,128)S(1)} custom-call(f32[4,32,32]{2,1,0:T(8,128)S(1)} %fusion.3), custom_call_target="Cholesky" | custom-call | tf_op jit(solution)/shard_map/jit(cholesky)/cholesky | solution.py:17
  49.3 0.1 compare_reduce_fusion
  49.5 0.1 select_bitcast_fusion
  49.5 9.8 %custom-call.8 = f32[4,1,32,32]{2,3,1,0:T(8,128)S(1)} custom-call(f32[4,1,32,32]{3,2,1,0:T(8,128)S(1)} %select_bitcast_fusion), custom_call_target="InvertDiagBlocksLowerTriangular" | custom-call | tf_op jit(solution)/shard_map/vmap()/triangular_solve | solution.py:10
  59.4 0.3 fusion.1
  59.7 0.0 copy-start.1
  59.7 23.9 %all_gather.3 = bf16[64,128,32]{1,2,0:T(8,128)(2,1)S(1)} all-gather(bf16[4,128,32]{1,2,0:T(8,128)(2,1)S(1)} %fusion.1), channel_id=1, replica_groups=mesh['sec'=16,'term'=2] {'sec'}, dimensions={0}, use_global_device_ids=true | all-gather | bytes 557056 | tf_op jit(solution)/shard_map/all_gather | solution.py:35
  83.6 0.7 gather_fusion
  84.3 1.4 %gather_fusion.1 = bf16[64,128,32]{1,2,0:T(8,128)(2,1)} fusion(bf16[64,128,32]{1,2,0:T(8,128)(2,1)S(1)} %all_gather.3, s32[1024]{0:T(1024)S(1)} %pad_clamp_fusion), kind=kCustom, calls=%fused_computation.1 | custom fusion | bytes 1048832 | tf_op jit(solution)/shard_map/gather | solution.py:36
  85.7 3.0 %fusion = f32[64,32,32]{2,1,0:T(8,128)} fusion(bf16[64,128,32]{1,2,0:T(8,128)(2,1)} %gather_fusion.1, bf16[64,128,32]{1,2,0:T(8,128)(2,1)S(1)} %gather_fusion, bf16[64,128,128]{2,1,0:T(8,128)(2,1)S(1)} %copy-done), kind=kOutput, calls=%fused_computation.3 | convolution fusion | flops 84148224 | bytes 3407872 | tf_op jit(solution)/shard_map/bkn,bnl->bkl/dot_general | solution.py:40
  88.6 2.6 %copy.16 = f32[64,32,32]{0,2,1:T(8,128)} copy(f32[64,32,32]{2,1,0:T(8,128)} %fusion) | data formatting | bytes 524288
  (14 shorter events, 0.1 us)
Async XLA Ops:
  7.2 78.5 %copy-start = (bf16[64,128,128]{2,1,0:T(8,128)(2,1)S(1)}, bf16[64,128,128]{2,1,0:T(8,128)(2,1)}, u32[]{:S(2)}) copy-start(bf16[64,128,128]{2,1,0:T(8,128)(2,1)} %param.11) | copy-start | bytes 6291460
  7.2 3.0 %copy-start.3 = (s32[64]{0:T(128)S(1)}, s32[64]{0:T(128)}, u32[]{:S(2)}) copy-start(s32[64]{0:T(128)} %param.10) | copy-start | bytes 772
  7.2 3.0 %copy-start.4 = (s32[64]{0:T(128)S(1)}, s32[64]{0:T(128)}, u32[]{:S(2)}) copy-start(s32[64]{0:T(128)} %param.9) | copy-start | bytes 772
  7.2 3.0 %copy-start.5 = (s32[4]{0:T(128)S(1)}, s32[4]{0:T(128)}, u32[]{:S(2)}) copy-start(s32[4]{0:T(128)} %param.8) | copy-start | bytes 52
  7.2 28.6 %copy-start.2 = (f32[4,128,32]{1,2,0:T(8,128)S(1)}, f32[4,128,32]{1,2,0:T(8,128)}, u32[]{:S(2)}) copy-start(f32[4,128,32]{1,2,0:T(8,128)} %param.7) | copy-start | bytes 196612
  7.2 28.5 %all-reduce.2.cloned.1.call-start = ((), (), s32[]{:S(2)}) async-start(), calls=%async_computation | async-start | bytes 524288 | tf_op jit(solution)/shard_map/psum | solution.py:30
  59.7 24.5 %copy-start.1 = (bf16[4,128,32]{1,2,0:T(8,128)(2,1)}, bf16[4,128,32]{1,2,0:T(8,128)(2,1)S(1)}, u32[]{:S(2)}) copy-start(bf16[4,128,32]{1,2,0:T(8,128)(2,1)S(1)} %fusion.1) | copy-start | bytes 98308
Sparse Core Ops, SparseCore 0:
  10.9 24.8 all-reduce.1
where the time goes:
time: 98.4 us; the launch traced here: 98.1 us
  waiting for transfers between devices  25.5 us (26%)
  blocking collectives  23.9 us (24%)
  other arithmetic  21.9 us (22%)
  between operations  14.2 us (14%)
  matrix products  7.79 us (8%)
  local copies, waits for them, and re-layouts  4.74 us (5%)
    psum x1, waiting for transfers between devices, shards(): density = lax.psum(partial_density, 'term')  25.5 us
    all_gather x1, blocking collectives, shards(): every_rot = lax.all_gather(rotation, 'sec', axis=0, tiled=True)  23.9 us
    another operation x4, other arithmetic, finish(): lower = jnp.linalg.cholesky(gram)  11.9 us
    another operation x3, other arithmetic, orthonormal(): lax.linalg.triangular_solve(lower_block, range_block, left_side=False, lo...  9.94 us
    dot_general x1, matrix products, shards(): jnp.einsum('bkn,bnl->bkl', half, right_rot, preferred_element_type=jnp.fl...  2.96 us
    dot_general x1, matrix products, shards(): jnp.einsum('smr,snr->smn', wavefunction, wavefunction, preferred_element_...  2.81 us
    unnamed x13, local copies, waits for them, and re-layouts  2.59 us
  transfers between devices with their start and end apart: 1, of which 1 were waited for; matrix products, arithmetic and copies ran while one was open for 0% of the time, Pallas kernels for 0%

commit v1 on v0

v1 whole, which is shorter than its diff:
```python
import functools

import jax
import jax.numpy as jnp
from jax import lax
from jax.experimental import pallas as pl
from jax.experimental.pallas import tpu as pltpu
from jax.sharding import PartitionSpec as P

HIGH = lax.Precision.HIGHEST
MESH = pl.DeviceIdType.MESH
F32 = jnp.float32


def dot_nt(a, b, precision=None):
    return lax.dot_general(
        a, b, (((1,), (1,)), ((), ())), precision=precision, preferred_element_type=F32
    )


def inverse_factors(gram, width):
    row = lax.broadcasted_iota(jnp.int32, gram.shape, 0)
    lane = lax.broadcasted_iota(jnp.int32, gram.shape, 1)
    first = lane // width * width
    eye = jnp.where(lane - first == row, 1.0, 0.0).astype(F32)
    scale = jnp.zeros_like(gram)
    for j in range(width):
        column = jnp.take_along_axis(gram, first + j, axis=1, mode="promise_in_bounds")
        root = lax.rsqrt(column[j : j + 1, :])
        scale = jnp.where(row == j, root, scale)
        if j + 1 < width:
            factor = jnp.where(row > j, column * root, 0.0)
            gram = gram - factor * (gram[j : j + 1, :] * root)
            eye = eye - factor * (eye[j : j + 1, :] * root)
    return eye * scale


def kernel(
    n_sec, n_term, kept_ref, left_ref, right_ref, wave_hbm, sketch_hbm, ops_hbm,
    rot_ref, out_ref,
    wave, sketch, ops, part, rt, every, half,
    wave_sem, sketch_sem, ops_sem, part_send, part_recv, send_sem, recv_sem,
):
    sectors, m, _ = wave.shape
    width = sketch.shape[1]
    blocks = ops.shape[0]
    sec = lax.axis_index("sec")
    term = lax.axis_index("term")
    core = lax.rem(sec, 2)
    side = lax.rem(sec // 2, 2)
    deep = sec // 4
    n_deep = n_sec // 4

    def place(a, b, c):
        return (a * 2 + b) * 2 + c

    terms = [lax.rem(term + t, n_term) for t in range(1, n_term)]
    deeps = [lax.rem(deep + t, n_deep) for t in range(1, n_deep)]
    side_peer = place(deep, 1 - side, core)
    core_peer = place(deep, side, 1 - core)

    waves = []
    for s in range(sectors):
        waves.append(pltpu.make_async_copy(wave_hbm.at[s], wave.at[s], wave_sem.at[s]))
        waves[-1].start()
    get_sketch = pltpu.make_async_copy(sketch_hbm, sketch, sketch_sem)
    get_sketch.start()
    get_ops = pltpu.make_async_copy(ops_hbm, ops, ops_sem)
    get_ops.start()

    barrier = pltpu.get_barrier_semaphore()
    for other in terms:
        pl.semaphore_signal(barrier, inc=1, device_id=(sec, other), device_id_type=MESH)
    peers = [place(a, side, core) for a in deeps] + [side_peer, core_peer]
    for other in peers:
        pl.semaphore_signal(barrier, inc=1, device_id=(other, term), device_id_type=MESH)

    get_sketch.wait()
    part_copies = []
    for s in range(sectors):
        waves[s].wait()
        w = wave[s]
        density = dot_nt(w, w)
        part[term, s] = jnp.dot(sketch[s], density, precision=HIGH, preferred_element_type=F32)
        if s == 0:
            pl.semaphore_wait(barrier, len(terms) + len(peers))
        for t, other in enumerate(terms):
            copy = pltpu.make_async_remote_copy(
                src_ref=part.at[term, s],
                dst_ref=part.at[term, s],
                send_sem=part_send.at[t, s],
                recv_sem=part_recv.at[term, s],
                device_id=(sec, other),
                device_id_type=MESH,
            )
            copy.start()
            part_copies.append(copy)
    for s in range(sectors):
        for other in terms:
            pltpu.make_async_remote_copy(
                src_ref=part.at[other, s],
                dst_ref=part.at[other, s],
                send_sem=part_send.at[0, s],
                recv_sem=part_recv.at[other, s],
                device_id=(sec, other),
                device_id_type=MESH,
            ).wait_recv()
    total = part[0]
    for t in range(1, n_term):
        total = total + part[t]
    total = total.reshape(sectors * width, m)

    full = dot_nt(total, total, HIGH)
    owner = lax.broadcasted_iota(jnp.int32, (width, sectors * width), 1) // width
    gram = full[:width]
    for s in range(1, sectors):
        gram = jnp.where(owner == s, full[s * width : (s + 1) * width], gram)
    inverse = inverse_factors(gram, width)
    spread = jnp.concatenate([jnp.where(owner == s, inverse, 0.0) for s in range(sectors)], axis=0)
    basis = jnp.dot(spread, total, precision=HIGH, preferred_element_type=F32)
    basis = basis.reshape(sectors, width, m)
    row = lax.broadcasted_iota(jnp.int32, (width, m), 0)
    for s in range(sectors):
        kept_rows = jnp.where(row < kept_ref[s], basis[s], 0.0).astype(jnp.bfloat16)
        rt[s] = kept_rows
        every[sec * sectors + s] = kept_rows

    sends = []

    def send(src, slot, device):
        copy = pltpu.make_async_remote_copy(
            src_ref=src,
            dst_ref=every.at[pl.ds(slot * sectors, sectors)],
            send_sem=send_sem.at[len(sends)],
            recv_sem=recv_sem.at[slot],
            device_id=(device, term),
            device_id_type=MESH,
        )
        copy.start()
        sends.append(copy)

    def arrived(slot):
        part_of = every.at[pl.ds(slot * sectors, sectors)]
        pltpu.make_async_remote_copy(
            src_ref=part_of,
            dst_ref=part_of,
            send_sem=send_sem.at[0],
            recv_sem=recv_sem.at[slot],
            device_id=(core_peer, term),
            device_id_type=MESH,
        ).wait_recv()
        return part_of

    for a in deeps:
        send(rt, sec, place(a, side, core))
    send(rt, sec, side_peer)
    send(rt, sec, core_peer)

    get_ops.wait()

    def left_side(start, stop):
        @pl.loop(start, stop, step=8)
        def _(first):
            for i in range(8):
                b = first + i
                rotated = jnp.dot(rt[lax.rem(left_ref[b], sectors)], ops[b], preferred_element_type=F32)
                half[b] = rotated.astype(jnp.bfloat16)

    left_side(0, blocks // 2)
    for a in deeps:
        slot = place(a, side, core)
        block = arrived(slot)
        send(block, slot, side_peer)
        send(block, slot, core_peer)
    left_side(blocks // 2, blocks)
    for a in [deep] + deeps:
        slot = place(a, 1 - side, core)
        block = arrived(slot)
        send(block, slot, core_peer)
    for s in range(sectors):
        rot_ref[s] = rt[s]
    for a in [deep] + deeps:
        for b in range(2):
            arrived(place(a, b, 1 - core))

    @pl.loop(0, blocks, step=8)
    def _(first):
        for i in range(8):
            b = first + i
            out_ref[b] = dot_nt(half[b], every[right_ref[b]])

    for copy in part_copies + sends:
        copy.wait_send()


def shards(n_sec, n_term, wavefunction, sketch, kept, left_ids, right_ids, operators):
    sectors, m, right = wavefunction.shape
    width = sketch.shape[2]
    blocks = operators.shape[0]
    n_deep = n_sec // 4
    n_sends = (n_deep - 1) + 2 + 2 * (n_deep - 1) + n_deep
    smem = pl.BlockSpec(memory_space=pltpu.SMEM)
    hbm = pl.BlockSpec(memory_space=pl.ANY)
    vmem = pl.BlockSpec(memory_space=pltpu.VMEM)
    dma = pltpu.SemaphoreType.DMA
    rotation, result = pl.pallas_call(
        functools.partial(kernel, n_sec, n_term),
        out_shape=(
            jax.ShapeDtypeStruct((sectors, width, m), jnp.bfloat16),
            jax.ShapeDtypeStruct((blocks, width, width), F32),
        ),
        in_specs=[smem, smem, smem, hbm, hbm, hbm],
        out_specs=(vmem, vmem),
        scratch_shapes=[
            pltpu.VMEM((sectors, m, right), jnp.bfloat16),
            pltpu.VMEM((sectors, width, m), F32),
            pltpu.VMEM((blocks, m, m), jnp.bfloat16),
            pltpu.VMEM((n_term, sectors, width, m), F32),
            pltpu.VMEM((sectors, width, m), jnp.bfloat16),
            pltpu.VMEM((n_sec * sectors, width, m), jnp.bfloat16),
            pltpu.VMEM((blocks, width, m), jnp.bfloat16),
            dma((sectors,)),
            dma,
            dma,
            dma((max(n_term - 1, 1), sectors)),
            dma((n_term, sectors)),
            dma((n_sends,)),
            dma((n_sec,)),
        ],
        compiler_params=pltpu.CompilerParams(
            collective_id=0, has_side_effects=True, vmem_limit_bytes=32 * 1024 * 1024
        ),
    )(kept, left_ids, right_ids, wavefunction, jnp.swapaxes(sketch, 1, 2), operators)
    return jnp.swapaxes(rotation, 1, 2), result


def solution(mesh):
    in_specs = (
        P("sec", None, "term"),
        P("sec", None, None),
        P("sec"),
        P(("sec", "term")),
        P(("sec", "term")),
        P(("sec", "term"), None, None),
    )
    out_specs = (P("sec", None, None), P(("sec", "term"), None, None))
    run = functools.partial(shards, mesh.shape["sec"], mesh.shape["term"])
    return jax.shard_map(run, mesh=mesh, in_specs=in_specs, out_specs=out_specs, check_vma=False)
```

time: 98.4 us -> 31.8 us (0.32)
  waiting for transfers between devices: 25.5 us -> 0 us
  blocking collectives: 23.9 us -> 0 us
  Pallas kernels: 0 us -> 23.3 us
  other arithmetic: 21.9 us -> 0 us
  between operations: 14.2 us -> 0.65 us
  matrix products: 7.79 us -> 0 us
  local copies, waits for them, and re-layouts: 4.74 us -> 7.62 us
    psum x1 -> x0, waiting for transfers between devices: 25.5 us -> none  [shards(): density = lax.psum(partial_density, 'term')]
    all_gather x1 -> x0, blocking collectives: 23.9 us -> none  [shards(): every_rot = lax.all_gather(rotation, 'sec', axis=0, tiled=True)]
    pallas_call x0 -> x1, Pallas kernels: none -> 23.3 us  [shards(): pl.pallas_call(functools.partial(kernel, n_sec, n_term), out_shape=(jax.S...]
    another operation x7 -> x0, other arithmetic: 21.8 us -> none  [the longest x4 11.9 us: finish(): lower = jnp.linalg.cholesky(gram)]
    dot_general x4 -> x0, matrix products: 7.48 us -> none  [the longest x1 2.96 us: shards(): jnp.einsum('bkn,bnl->bkl', half, right_rot, preferred_element_type=jnp.fl...]
    unnamed x13 -> x14, local copies, waits for them, and re-layouts: 2.59 us -> 7.62 us
    gather x2 -> x0, local copies, waits for them, and re-layouts: 2.07 us -> none  [the longest x1 1.42 us: shards(): right_rot = every_rot[right_ids]]
  transfers between devices with their start and end apart: 1 -> 0, of which waited for: 1 -> 0; matrix products, arithmetic and copies ran while one was open for 0% -> 0% of each run, Pallas kernels for 0% -> 0%
where the time goes in v1:
time: 31.8 us; the launch traced here: 31.5 us
  Pallas kernels  23.3 us (73%)
  local copies, waits for them, and re-layouts  7.62 us (24%)
  between operations  0.65 us (2%)
    pallas_call x1, Pallas kernels, shards(): pl.pallas_call(functools.partial(kernel, n_sec, n_term), out_shape=(jax.S...  23.3 us
    unnamed x14, local copies, waits for them, and re-layouts  7.62 us

profile of v1, /device:TPU:1, one launch (start us, length us, event | category | flops | bytes accessed | tf_op | source)
XLA Modules:
  0.0 31.5 jit_solution(9266357352579223083)
XLA Ops:
  0.6 0.0 copy-start
  0.6 1.6 %copy-done = bf16[64,128,128]{2,1,0:T(8,128)(2,1)S(1)} copy-done((bf16[64,128,128]{2,1,0:T(8,128)(2,1)S(1)}, bf16[64,128,128]{2,1,0:T(8,128)(2,1)}, u32[]{:S(2)}) %copy-start) | copy-done | bytes 2097176
  2.2 0.0 copy-start.1
  2.2 1.2 %copy-done.1 = bf16[4,128,1024]{2,1,0:T(8,128)(2,1)S(1)} copy-done((bf16[4,128,1024]{2,1,0:T(8,128)(2,1)S(1)}, bf16[4,128,1024]{2,1,0:T(8,128)(2,1)}, u32[]{:S(2)}) %copy-start.1) | copy-done | bytes 1048600
  3.4 0.0 copy-start.2
  3.5 0.8 %copy-done.2 = f32[4,128,32]{1,2,0:T(8,128)S(1)} copy-done((f32[4,128,32]{1,2,0:T(8,128)S(1)}, f32[4,128,32]{1,2,0:T(8,128)}, u32[]{:S(2)}) %copy-start.2) | copy-done | bytes 65560
  4.3 0.0 copy-start.3
  4.3 0.7 %copy-done.3 = s32[4]{0:T(128)S(1)} copy-done((s32[4]{0:T(128)S(1)}, s32[4]{0:T(128)}, u32[]{:S(2)}) %copy-start.3) | copy-done | bytes 40
  4.9 0.0 copy-start.4
  4.9 0.7 %copy-done.4 = s32[64]{0:T(128)S(1)} copy-done((s32[64]{0:T(128)S(1)}, s32[64]{0:T(128)}, u32[]{:S(2)}) %copy-start.4) | copy-done | bytes 280
  5.6 0.0 copy-start.5
  5.6 0.7 %copy-done.5 = s32[64]{0:T(128)S(1)} copy-done((s32[64]{0:T(128)S(1)}, s32[64]{0:T(128)}, u32[]{:S(2)}) %copy-start.5) | copy-done | bytes 280
  6.3 23.3 %shard_map.77 = (bf16[4,32,128]{2,1,0:T(8,128)(2,1)S(1)}, f32[64,32,32]{2,1,0:T(8,128)S(1)}) custom-call(s32[4]{0:T(128)S(1)} %copy-done.3, s32[64]{0:T(128)S(1)} %copy-done.4, s32[64]{0:T(128)S(1)} %copy-done.5, bf16[4,128,1024]{2,1,0:T(8,128)(2,1)S(1)} %copy-done.1, f32[4,32,128]{2,1,0:T(8,128)S(1)} %bitcast.2, bf16[64,128,128]{2,1,0:T(8,128)(2,1)S(1)} %copy-done), custom_call_target="tpu_custom_call" | custom-call | tf_op jit(solution)/shard_map/pallas_call | solution.py:206
  29.5 1.4 %copy.8 = f32[64,32,32]{0,2,1:T(8,128)} copy(f32[64,32,32]{2,1,0:T(8,128)S(1)} %get-tuple-element.7) | data formatting | bytes 524288
  30.9 0.6 %copy.10 = bf16[4,128,32]{1,2,0:T(8,128)(2,1)} copy(bf16[4,128,32]{1,2,0:T(8,128)(2,1)S(1)} %bitcast.3) | data formatting | bytes 65536
Async XLA Ops:
  0.6 1.6 %copy-start = (bf16[64,128,128]{2,1,0:T(8,128)(2,1)S(1)}, bf16[64,128,128]{2,1,0:T(8,128)(2,1)}, u32[]{:S(2)}) copy-start(bf16[64,128,128]{2,1,0:T(8,128)(2,1)} %ops_hbm.1) | copy-start | bytes 6291460
  2.2 1.2 %copy-start.1 = (bf16[4,128,1024]{2,1,0:T(8,128)(2,1)S(1)}, bf16[4,128,1024]{2,1,0:T(8,128)(2,1)}, u32[]{:S(2)}) copy-start(bf16[4,128,1024]{2,1,0:T(8,128)(2,1)} %wave_hbm.1) | copy-start | bytes 3145732
  3.4 0.8 %copy-start.2 = (f32[4,128,32]{1,2,0:T(8,128)S(1)}, f32[4,128,32]{1,2,0:T(8,128)}, u32[]{:S(2)}) copy-start(f32[4,128,32]{1,2,0:T(8,128)} %param.7) | copy-start | bytes 196612
  4.3 0.7 %copy-start.3 = (s32[4]{0:T(128)S(1)}, s32[4]{0:T(128)}, u32[]{:S(2)}) copy-start(s32[4]{0:T(128)} %kept_ref.1) | copy-start | bytes 52
  4.9 0.7 %copy-start.4 = (s32[64]{0:T(128)S(1)}, s32[64]{0:T(128)}, u32[]{:S(2)}) copy-start(s32[64]{0:T(128)} %left_ref.1) | copy-start | bytes 772
  5.6 0.7 %copy-start.5 = (s32[64]{0:T(128)S(1)}, s32[64]{0:T(128)}, u32[]{:S(2)}) copy-start(s32[64]{0:T(128)} %right_ref.1) | copy-start | bytes 772

commit v2 on v1

--- a/solution.py
+++ b/solution.py
@@ -36,9 +36,9 @@
 
 
 def kernel(
-    n_sec, n_term, kept_ref, left_ref, right_ref, wave_hbm, sketch_hbm, ops_hbm,
+    n_sec, n_term, kept_hbm, left_hbm, right_hbm, wave_hbm, sketch_hbm, ops_hbm,
     rot_ref, out_ref,
-    wave, sketch, ops, part, rt, every, half,
+    kept_ref, left_ref, right_ref, ids_sem, wave, sketch, ops, part, rt, every, half,
     wave_sem, sketch_sem, ops_sem, part_send, part_recv, send_sem, recv_sem,
 ):
     sectors, m, _ = wave.shape
@@ -67,6 +67,10 @@
     get_sketch.start()
     get_ops = pltpu.make_async_copy(ops_hbm, ops, ops_sem)
     get_ops.start()
+    get_ids = []
+    for i, (src, dst) in enumerate(((kept_hbm, kept_ref), (left_hbm, left_ref), (right_hbm, right_ref))):
+        get_ids.append(pltpu.make_async_copy(src, dst, ids_sem.at[i]))
+        get_ids[-1].start()
 
     barrier = pltpu.get_barrier_semaphore()
     for other in terms:
@@ -105,6 +109,8 @@
                 device_id=(sec, other),
                 device_id_type=MESH,
             ).wait_recv()
+    for copy in get_ids:
+        copy.wait()
     total = part[0]
     for t in range(1, n_term):
         total = total + part[t]
@@ -199,7 +205,6 @@
     blocks = operators.shape[0]
     n_deep = n_sec // 4
     n_sends = (n_deep - 1) + 2 + 2 * (n_deep - 1) + n_deep
-    smem = pl.BlockSpec(memory_space=pltpu.SMEM)
     hbm = pl.BlockSpec(memory_space=pl.ANY)
     vmem = pl.BlockSpec(memory_space=pltpu.VMEM)
     dma = pltpu.SemaphoreType.DMA
@@ -209,9 +214,13 @@
             jax.ShapeDtypeStruct((sectors, width, m), jnp.bfloat16),
             jax.ShapeDtypeStruct((blocks, width, width), F32),
         ),
-        in_specs=[smem, smem, smem, hbm, hbm, hbm],
+        in_specs=[hbm] * 6,
         out_specs=(vmem, vmem),
         scratch_shapes=[
+            pltpu.SMEM((sectors,), jnp.int32),
+            pltpu.SMEM((blocks,), jnp.int32),
+            pltpu.SMEM((blocks,), jnp.int32),
+            pltpu.SemaphoreType.DMA((3,)),
             pltpu.VMEM((sectors, m, right), jnp.bfloat16),
             pltpu.VMEM((sectors, width, m), F32),
             pltpu.VMEM((blocks, m, m), jnp.bfloat16),
@@ -228,7 +237,7 @@
             dma((n_sec,)),
         ],
         compiler_params=pltpu.CompilerParams(
-            collective_id=0, has_side_effects=True, vmem_limit_bytes=32 * 1024 * 1024
+            collective_id=0, has_side_effects=True, vmem_limit_bytes=62 * 1024 * 1024
         ),
     )(kept, left_ids, right_ids, wavefunction, jnp.swapaxes(sketch, 1, 2), operators)
     return jnp.swapaxes(rotation, 1, 2), result

time: 31.8 us -> 28.3 us (0.89)
  local copies, waits for them, and re-layouts: 7.62 us -> 3.94 us
    unnamed x14 -> x2, local copies, waits for them, and re-layouts: 7.62 us -> 3.94 us
where the time goes in v2:
time: 28.3 us; the launch traced here: 28 us
  Pallas kernels  23.5 us (83%)
  local copies, waits for them, and re-layouts  3.94 us (14%)
  between operations  0.64 us (2%)
    pallas_call x1, Pallas kernels, shards(): pl.pallas_call(functools.partial(kernel, n_sec, n_term), out_shape=(jax.S...  23.5 us
    unnamed x2, local copies, waits for them, and re-layouts  3.94 us

profile of v2, /device:TPU:1, one launch (start us, length us, event | category | flops | bytes accessed | tf_op | source)
XLA Modules:
  0.0 28.0 jit_solution(15942795701935040470)
XLA Ops:
  0.6 23.5 %shard_map.77 = (bf16[4,32,128]{2,1,0:T(8,128)(2,1)}, f32[64,32,32]{2,1,0:T(8,128)}) custom-call(s32[4]{0:T(128)} %kept_hbm.1, s32[64]{0:T(128)} %left_hbm.1, s32[64]{0:T(128)} %right_hbm.1, bf16[4,128,1024]{2,1,0:T(8,128)(2,1)} %wave_hbm.1, f32[4,32,128]{2,1,0:T(8,128)} %bitcast.2, bf16[64,128,128]{2,1,0:T(8,128)(2,1)} %ops_hbm.1), custom_call_target="tpu_custom_call" | custom-call | tf_op jit(solution)/shard_map/pallas_call | solution.py:211
  24.1 2.6 %copy.8 = f32[64,32,32]{0,2,1:T(8,128)} copy(f32[64,32,32]{2,1,0:T(8,128)} %get-tuple-element.7) | data formatting | bytes 524288
  26.7 1.4 %copy.10 = bf16[4,128,32]{1,2,0:T(8,128)(2,1)} copy(bf16[4,128,32]{1,2,0:T(8,128)(2,1)} %bitcast.3) | data formatting | bytes 65536

commit v3 on v2

--- a/solution.py
+++ b/solution.py
@@ -36,9 +36,9 @@
 
 
 def kernel(
-    n_sec, n_term, kept_hbm, left_hbm, right_hbm, wave_hbm, sketch_hbm, ops_hbm,
-    rot_ref, out_ref,
-    kept_ref, left_ref, right_ref, ids_sem, wave, sketch, ops, part, rt, every, half,
+    n_sec, n_term, kept_hbm, left_hbm, wave_hbm, sketch_hbm, ops_hbm,
+    rot_out, half_out, every_out,
+    kept_ref, left_ref, ids_sem, out_sem, wave, sketch, ops, part, rt, every, half,
     wave_sem, sketch_sem, ops_sem, part_send, part_recv, send_sem, recv_sem,
 ):
     sectors, m, _ = wave.shape
@@ -68,7 +68,7 @@
     get_ops = pltpu.make_async_copy(ops_hbm, ops, ops_sem)
     get_ops.start()
     get_ids = []
-    for i, (src, dst) in enumerate(((kept_hbm, kept_ref), (left_hbm, left_ref), (right_hbm, right_ref))):
+    for i, (src, dst) in enumerate(((kept_hbm, kept_ref), (left_hbm, left_ref))):
         get_ids.append(pltpu.make_async_copy(src, dst, ids_sem.at[i]))
         get_ids[-1].start()
 
@@ -162,6 +162,8 @@
     send(rt, sec, side_peer)
     send(rt, sec, core_peer)
 
+    outs = [pltpu.make_async_copy(rt, rot_out, out_sem.at[0])]
+    outs[0].start()
     get_ops.wait()
 
     def left_side(start, stop):
@@ -179,24 +181,37 @@
         send(block, slot, side_peer)
         send(block, slot, core_peer)
     left_side(blocks // 2, blocks)
+    outs.append(pltpu.make_async_copy(half, half_out, out_sem.at[1]))
+    outs[1].start()
     for a in [deep] + deeps:
         slot = place(a, 1 - side, core)
         block = arrived(slot)
         send(block, slot, core_peer)
-    for s in range(sectors):
-        rot_ref[s] = rt[s]
     for a in [deep] + deeps:
         for b in range(2):
             arrived(place(a, b, 1 - core))
+
+    outs.append(pltpu.make_async_copy(every, every_out, out_sem.at[2]))
+    outs[2].start()
+    for copy in outs:
+        copy.wait()
+    for copy in part_copies + sends:
+        copy.wait_send()
+
+
+def right_kernel(right_ref, rot_in, half, every, rot_out, out_ref, result):
+    blocks, width, _ = half.shape
+    rot_out[...] = rot_in[...]
 
     @pl.loop(0, blocks, step=8)
     def _(first):
         for i in range(8):
             b = first + i
-            out_ref[b] = dot_nt(half[b], every[right_ref[b]])
-
-    for copy in part_copies + sends:
-        copy.wait_send()
+            rows = pl.ds(pl.multiple_of(b * width, width), width)
+            result[rows, :width] = dot_nt(half[b], every[right_ref[b]])
+
+    for k in range(width):
+        out_ref[k] = result[pl.ds(k, blocks, stride=width), :][:, :width].T
 
 
 def shards(n_sec, n_term, wavefunction, sketch, kept, left_ids, right_ids, operators):
@@ -208,18 +223,19 @@
     hbm = pl.BlockSpec(memory_space=pl.ANY)
     vmem = pl.BlockSpec(memory_space=pltpu.VMEM)
     dma = pltpu.SemaphoreType.DMA
-    rotation, result = pl.pallas_call(
+    rotation, half, every = pl.pallas_call(
         functools.partial(kernel, n_sec, n_term),
         out_shape=(
             jax.ShapeDtypeStruct((sectors, width, m), jnp.bfloat16),
-            jax.ShapeDtypeStruct((blocks, width, width), F32),
+            jax.ShapeDtypeStruct((blocks, width, m), jnp.bfloat16),
+            jax.ShapeDtypeStruct((n_sec * sectors, width, m), jnp.bfloat16),
         ),
-        in_specs=[hbm] * 6,
-        out_specs=(vmem, vmem),
+        in_specs=[hbm] * 5,
+        out_specs=(hbm, hbm, hbm),
         scratch_shapes=[
             pltpu.SMEM((sectors,), jnp.int32),
             pltpu.SMEM((blocks,), jnp.int32),
-            pltpu.SMEM((blocks,), jnp.int32),
+            pltpu.SemaphoreType.DMA((2,)),
             pltpu.SemaphoreType.DMA((3,)),
             pltpu.VMEM((sectors, m, right), jnp.bfloat16),
             pltpu.VMEM((sectors, width, m), F32),
@@ -239,8 +255,19 @@
         compiler_params=pltpu.CompilerParams(
             collective_id=0, has_side_effects=True, vmem_limit_bytes=62 * 1024 * 1024
         ),
-    )(kept, left_ids, right_ids, wavefunction, jnp.swapaxes(sketch, 1, 2), operators)
-    return jnp.swapaxes(rotation, 1, 2), result
+    )(kept, left_ids, wavefunction, jnp.swapaxes(sketch, 1, 2), operators)
+    rotation, result = pl.pallas_call(
+        right_kernel,
+        out_shape=(
+            jax.ShapeDtypeStruct((sectors, width, m), jnp.bfloat16),
+            jax.ShapeDtypeStruct((width, width, blocks), F32),
+        ),
+        in_specs=[pl.BlockSpec(memory_space=pltpu.SMEM), vmem, vmem, vmem],
+        out_specs=(vmem, vmem),
+        scratch_shapes=[pltpu.VMEM((blocks * width, 128), F32)],
+        compiler_params=pltpu.CompilerParams(vmem_limit_bytes=62 * 1024 * 1024),
+    )(right_ids, rotation, half, every)
+    return jnp.swapaxes(rotation, 1, 2), jnp.transpose(result, (2, 0, 1))
 
 
 def solution(mesh):

time: 28.3 us -> 26.7 us (0.943)
  local copies, waits for them, and re-layouts: 3.94 us -> 0 us
  Pallas kernels: 23.5 us -> 25.9 us
    pallas_call x0 -> x1, Pallas kernels: none -> 3.98 us  [shards(): pl.pallas_call(right_kernel, out_shape=(jax.ShapeDtypeStruct((sectors, wi...]
    unnamed x2 -> x0, local copies, waits for them, and re-layouts: 3.94 us -> none
    pallas_call x1, Pallas kernels: 23.5 us -> 22 us  [shards(): pl.pallas_call(functools.partial(kernel, n_sec, n_term), out_shape=(jax.S...]
where the time goes in v3:
time: 26.7 us; the launch traced here: 26.6 us
  Pallas kernels  25.9 us (97%)
  between operations  0.64 us (2%)
    pallas_call x1, Pallas kernels, shards(): pl.pallas_call(functools.partial(kernel, n_sec, n_term), out_shape=(jax.S...  22 us
    pallas_call x1, Pallas kernels, shards(): pl.pallas_call(right_kernel, out_shape=(jax.ShapeDtypeStruct((sectors, wi...  3.98 us

profile of v3, /device:TPU:1, one launch (start us, length us, event | category | flops | bytes accessed | tf_op | source)
XLA Modules:
  0.0 26.6 jit_solution(1873239912784868480)
XLA Ops:
  0.6 22.0 %shard_map.77 = (bf16[4,32,128]{2,1,0:T(8,128)(2,1)}, bf16[64,32,128]{2,1,0:T(8,128)(2,1)}, bf16[64,32,128]{2,1,0:T(8,128)(2,1)}) custom-call(s32[4]{0:T(128)} %kept_hbm.1, s32[64]{0:T(128)} %left_hbm.1, bf16[4,128,1024]{2,1,0:T(8,128)(2,1)} %wave_hbm.1, f32[4,32,128]{2,1,0:T(8,128)} %bitcast.3, bf16[64,128,128]{2,1,0:T(8,128)(2,1)} %ops_hbm.1), custom_call_target="tpu_custom_call" | custom-call | tf_op jit(solution)/shard_map/pallas_call | solution.py:226
  22.6 4.0 %shard_map.78 = (bf16[4,32,128]{2,1,0:T(8,128)(2,1)}, f32[32,32,64]{2,1,0:T(8,128)}) custom-call(s32[64]{0:T(128)} %right_ref.1, bf16[4,32,128]{2,1,0:T(8,128)(2,1)} %get-tuple-element.7.rot_in, bf16[64,32,128]{2,1,0:T(8,128)(2,1)} %get-tuple-element.8.half, bf16[64,32,128]{2,1,0:T(8,128)(2,1)} %get-tuple-element.9.every), custom_call_target="tpu_custom_call" | custom-call | tf_op jit(solution)/shard_map/pallas_call | solution.py:259

commit v4 on v3

--- a/solution.py
+++ b/solution.py
@@ -145,6 +145,11 @@
         copy.start()
         sends.append(copy)
 
+    def keep(slot):
+        rows = pl.ds(slot * sectors, sectors)
+        outs.append(pltpu.make_async_copy(every.at[rows], every_out.at[rows], out_sem.at[len(outs)]))
+        outs[-1].start()
+
     def arrived(slot):
         part_of = every.at[pl.ds(slot * sectors, sectors)]
         pltpu.make_async_remote_copy(
@@ -155,6 +160,7 @@
             device_id=(core_peer, term),
             device_id_type=MESH,
         ).wait_recv()
+        keep(slot)
         return part_of
 
     for a in deeps:
@@ -164,6 +170,7 @@
 
     outs = [pltpu.make_async_copy(rt, rot_out, out_sem.at[0])]
     outs[0].start()
+    keep(sec)
     get_ops.wait()
 
     def left_side(start, stop):
@@ -181,8 +188,8 @@
         send(block, slot, side_peer)
         send(block, slot, core_peer)
     left_side(blocks // 2, blocks)
-    outs.append(pltpu.make_async_copy(half, half_out, out_sem.at[1]))
-    outs[1].start()
+    outs.append(pltpu.make_async_copy(half, half_out, out_sem.at[len(outs)]))
+    outs[-1].start()
     for a in [deep] + deeps:
         slot = place(a, 1 - side, core)
         block = arrived(slot)
@@ -191,27 +198,37 @@
         for b in range(2):
             arrived(place(a, b, 1 - core))
 
-    outs.append(pltpu.make_async_copy(every, every_out, out_sem.at[2]))
-    outs[2].start()
     for copy in outs:
         copy.wait()
     for copy in part_copies + sends:
         copy.wait_send()
 
 
-def right_kernel(right_ref, rot_in, half, every, rot_out, out_ref, result):
+def right_kernel(
+    right_hbm, rot_in, half_hbm, every_hbm, rot_out, out_hbm,
+    right_ref, half, every, result, flipped, in_sem, out_sem,
+):
     blocks, width, _ = half.shape
-    rot_out[...] = rot_in[...]
-
-    @pl.loop(0, blocks, step=8)
-    def _(first):
-        for i in range(8):
-            b = first + i
-            rows = pl.ds(pl.multiple_of(b * width, width), width)
-            result[rows, :width] = dot_nt(half[b], every[right_ref[b]])
-
-    for k in range(width):
-        out_ref[k] = result[pl.ds(k, blocks, stride=width), :][:, :width].T
+    pairs = ((right_hbm, right_ref), (half_hbm, half), (every_hbm, every), (rot_in, rot_out))
+    copies = [pltpu.make_async_copy(src, dst, in_sem.at[i]) for i, (src, dst) in enumerate(pairs)]
+    for copy in copies:
+        copy.start()
+    for copy in copies[:3]:
+        copy.wait()
+
+    for b in range(blocks):
+        result[b * width : (b + 1) * width, :width] = dot_nt(half[b], every[right_ref[b]])
+
+    step = width // 4
+    outs = []
+    for part in range(4):
+        for k in range(part * step, (part + 1) * step):
+            flipped[k] = result[pl.ds(k, blocks, stride=width), :][:, :width].T
+        rows = pl.ds(part * step, step)
+        outs.append(pltpu.make_async_copy(flipped.at[rows], out_hbm.at[rows], out_sem.at[part]))
+        outs[-1].start()
+    for copy in outs + copies[3:]:
+        copy.wait()
 
 
 def shards(n_sec, n_term, wavefunction, sketch, kept, left_ids, right_ids, operators):
@@ -221,7 +238,6 @@
     n_deep = n_sec // 4
     n_sends = (n_deep - 1) + 2 + 2 * (n_deep - 1) + n_deep
     hbm = pl.BlockSpec(memory_space=pl.ANY)
-    vmem = pl.BlockSpec(memory_space=pltpu.VMEM)
     dma = pltpu.SemaphoreType.DMA
     rotation, half, every = pl.pallas_call(
         functools.partial(kernel, n_sec, n_term),
@@ -236,7 +252,7 @@
             pltpu.SMEM((sectors,), jnp.int32),
             pltpu.SMEM((blocks,), jnp.int32),
             pltpu.SemaphoreType.DMA((2,)),
-            pltpu.SemaphoreType.DMA((3,)),
+            pltpu.SemaphoreType.DMA((n_sec + 2,)),
             pltpu.VMEM((sectors, m, right), jnp.bfloat16),
             pltpu.VMEM((sectors, width, m), F32),
             pltpu.VMEM((blocks, m, m), jnp.bfloat16),
@@ -262,9 +278,17 @@
             jax.ShapeDtypeStruct((sectors, width, m), jnp.bfloat16),
             jax.ShapeDtypeStruct((width, width, blocks), F32),
         ),
-        in_specs=[pl.BlockSpec(memory_space=pltpu.SMEM), vmem, vmem, vmem],
-        out_specs=(vmem, vmem),
-        scratch_shapes=[pltpu.VMEM((blocks * width, 128), F32)],
+        in_specs=[hbm] * 4,
+        out_specs=(hbm, hbm),
+        scratch_shapes=[
+            pltpu.SMEM((blocks,), jnp.int32),
+            pltpu.VMEM((blocks, width, m), jnp.bfloat16),
+            pltpu.VMEM((n_sec * sectors, width, m), jnp.bfloat16),
+            pltpu.VMEM((blocks * width, 128), F32),
+            pltpu.VMEM((width, width, blocks), F32),
+            dma((4,)),
+            dma((4,)),
+        ],
         compiler_params=pltpu.CompilerParams(vmem_limit_bytes=62 * 1024 * 1024),
     )(right_ids, rotation, half, every)
     return jnp.swapaxes(rotation, 1, 2), jnp.transpose(result, (2, 0, 1))

time: 26.7 us -> 25.7 us (0.963)
  Pallas kernels: 25.9 us -> 24.9 us
    pallas_call x1, Pallas kernels: 3.98 us -> 2.99 us  [shards(): pl.pallas_call(right_kernel, out_shape=(jax.ShapeDtypeStruct((sectors, wi...]
where the time goes in v4:
time: 25.7 us; the launch traced here: 25.5 us
  Pallas kernels  24.9 us (97%)
  between operations  0.64 us (2%)
    pallas_call x1, Pallas kernels, shards(): pl.pallas_call(functools.partial(kernel, n_sec, n_term), out_shape=(jax.S...  21.9 us
    pallas_call x1, Pallas kernels, shards(): pl.pallas_call(right_kernel, out_shape=(jax.ShapeDtypeStruct((sectors, wi...  2.99 us

profile of v4, /device:TPU:1, one launch (start us, length us, event | category | flops | bytes accessed | tf_op | source)
XLA Modules:
  0.0 25.5 jit_solution(1499581088388307114)
XLA Ops:
  0.6 21.9 %shard_map.77 = (bf16[4,32,128]{2,1,0:T(8,128)(2,1)}, bf16[64,32,128]{2,1,0:T(8,128)(2,1)}, bf16[64,32,128]{2,1,0:T(8,128)(2,1)}) custom-call(s32[4]{0:T(128)} %kept_hbm.1, s32[64]{0:T(128)} %left_hbm.1, bf16[4,128,1024]{2,1,0:T(8,128)(2,1)} %wave_hbm.1, f32[4,32,128]{2,1,0:T(8,128)} %bitcast.3, bf16[64,128,128]{2,1,0:T(8,128)(2,1)} %ops_hbm.1), custom_call_target="tpu_custom_call" | custom-call | tf_op jit(solution)/shard_map/pallas_call | solution.py:242
  22.5 3.0 %shard_map.78 = (bf16[4,32,128]{2,1,0:T(8,128)(2,1)}, f32[32,32,64]{2,1,0:T(8,128)}) custom-call(s32[64]{0:T(128)} %right_hbm.1, bf16[4,32,128]{2,1,0:T(8,128)(2,1)} %get-tuple-element.7.rot_in, bf16[64,32,128]{2,1,0:T(8,128)(2,1)} %get-tuple-element.8.half_hbm, bf16[64,32,128]{2,1,0:T(8,128)(2,1)} %get-tuple-element.9.every_hbm), custom_call_target="tpu_custom_call" | custom-call | tf_op jit(solution)/shard_map/pallas_call | solution.py:275

commit v5 on v4

--- a/solution.py
+++ b/solution.py
@@ -181,13 +181,15 @@
                 rotated = jnp.dot(rt[lax.rem(left_ref[b], sectors)], ops[b], preferred_element_type=F32)
                 half[b] = rotated.astype(jnp.bfloat16)
 
-    left_side(0, blocks // 2)
+    left_side(0, blocks // 4)
     for a in deeps:
         slot = place(a, side, core)
         block = arrived(slot)
         send(block, slot, side_peer)
-        send(block, slot, core_peer)
-    left_side(blocks // 2, blocks)
+    for a in deeps:
+        slot = place(a, side, core)
+        send(every.at[pl.ds(slot * sectors, sectors)], slot, core_peer)
+    left_side(blocks // 4, blocks)
     outs.append(pltpu.make_async_copy(half, half_out, out_sem.at[len(outs)]))
     outs[-1].start()
     for a in [deep] + deeps:

time: 25.7 us -> 25.7 us (level)
  no operation moved by 1% of the time
where the time goes in v5:
time: 25.7 us; the launch traced here: 25.5 us
  Pallas kernels  24.9 us (97%)
  between operations  0.64 us (2%)
    pallas_call x1, Pallas kernels, shards(): pl.pallas_call(functools.partial(kernel, n_sec, n_term), out_shape=(jax.S...  21.9 us
    pallas_call x1, Pallas kernels, shards(): pl.pallas_call(right_kernel, out_shape=(jax.ShapeDtypeStruct((sectors, wi...  2.99 us

profile of v5, /device:TPU:1, one launch (start us, length us, event | category | flops | bytes accessed | tf_op | source)
XLA Modules:
  0.0 25.5 jit_solution(12468516145478403200)
XLA Ops:
  0.6 21.9 %shard_map.77 = (bf16[4,32,128]{2,1,0:T(8,128)(2,1)}, bf16[64,32,128]{2,1,0:T(8,128)(2,1)}, bf16[64,32,128]{2,1,0:T(8,128)(2,1)}) custom-call(s32[4]{0:T(128)} %kept_hbm.1, s32[64]{0:T(128)} %left_hbm.1, bf16[4,128,1024]{2,1,0:T(8,128)(2,1)} %wave_hbm.1, f32[4,32,128]{2,1,0:T(8,128)} %bitcast.3, bf16[64,128,128]{2,1,0:T(8,128)(2,1)} %ops_hbm.1), custom_call_target="tpu_custom_call" | custom-call | tf_op jit(solution)/shard_map/pallas_call | solution.py:244
  22.5 3.0 %shard_map.78 = (bf16[4,32,128]{2,1,0:T(8,128)(2,1)}, f32[32,32,64]{2,1,0:T(8,128)}) custom-call(s32[64]{0:T(128)} %right_hbm.1, bf16[4,32,128]{2,1,0:T(8,128)(2,1)} %get-tuple-element.7.rot_in, bf16[64,32,128]{2,1,0:T(8,128)(2,1)} %get-tuple-element.8.half_hbm, bf16[64,32,128]{2,1,0:T(8,128)(2,1)} %get-tuple-element.9.every_hbm), custom_call_target="tpu_custom_call" | custom-call | tf_op jit(solution)/shard_map/pallas_call | solution.py:277
